TPU v7x, 512 devices: a whole 4x4x16 slice. The times are simulated.
512 devices in a mesh: frames: 128 (over y, x, z_hi, core), rows: 4 (over z_lo).
Axes of the slice: x: 4, y: 4, z: 16 (z_hi: 4, z_lo: 4; z = z_hi * 4 + z_lo), core: 2. Of those that a mesh axis runs over, the one named last changes fastest.
Arguments:
- act: bfloat16 [384, 256, 4, 128], P(None, 'frames', 'rows'), may hold values from -600 to 600, as said below
- cotangent: bfloat16 [96, 256, 4, 128], P(None, 'frames', 'rows'), may hold values from -6 to 6
- kernel: bfloat16 [27, 96, 384], replicated, may hold values from -0.0625 to 0.0625
- gamma: float32 [384], replicated, may hold values from 0.5 to 1.5
- beta: float32 [384], replicated, may hold values from -3 to 3
Outputs:
- act_grad: bfloat16 [384, 256, 4, 128], P(None, 'frames', 'rows')
- kernel_grad: float32 [27, 36864], P(None, ('frames', 'rows'))
- gamma_grad: float32 [384], replicated
- beta_grad: float32 [384], replicated
- group_mean: float32 [16, 32], replicated
- group_rstd: float32 [16, 32], replicated
Inputs may be any that keep to these rules, and one draw needn't show every extreme that they name: act has channel-dependent scales and offsets.
All inputs are finite; a program needn't handle non-finite values.
Results may differ from a plain program's by a relative error of at most 0.003.
Values may be sent and summed in bfloat16 or wider, within the bound.
A program may use at most 128 MiB of HBM per device.

v0:
```python
import jax
import jax.numpy as jnp
from jax import lax
from jax.sharding import PartitionSpec as P

GROUPS = 32
KERNEL = 3
CLIP_FRAMES = 16


EPS = 1e-06


def passed_along(array, axis, by):
    count = lax.axis_size(axis)
    pairs = [(i, i + by) for i in range(count) if 0 <= i + by < count]
    return lax.ppermute(array, axis, pairs)


def extended(block, sides, width):
    for axis, dim in sides:
        count = lax.axis_size(axis)
        forward = [(i, i + 1) for i in range(count - 1)]
        backward = [(target, source) for source, target in forward]
        low = lax.ppermute(
            lax.slice_in_dim(block, block.shape[dim] - width, None, axis=dim), axis, forward
        )
        high = lax.ppermute(lax.slice_in_dim(block, 0, width, axis=dim), axis, backward)
        block = jnp.concatenate([low, block, high], axis=dim)
    return block


def normalize(block, group_mean, group_rstd, gamma, beta):
    full_shape = block.shape
    grouped = block.astype(jnp.float32).reshape(GROUPS, full_shape[0] // GROUPS, -1)
    normed = ((grouped - group_mean[:, None, None]) * group_rstd[:, None, None]).reshape(full_shape)
    shaped = normed * gamma[:, None, None, None] + beta[:, None, None, None]
    return (normed, shaped)


def select_clip(table, picker):
    return jnp.sum(picker[:, None] * table, axis=0)


def on_device(act, cotangent, kernel, gamma, beta):
    channels, frames_dev, rows_dev, columns = act.shape
    outputs_ch = cotangent.shape[0]
    causal_lead = KERNEL - 1
    margin = (KERNEL - 1) // 2
    clip_span = CLIP_FRAMES // frames_dev
    clip_count = lax.axis_size("frames") // clip_span
    frame_place = lax.axis_index("frames")
    clip_number = frame_place // clip_span
    clip_step = frame_place % clip_span
    picker = (jnp.arange(clip_count) == clip_number).astype(jnp.float32)
    cells_dev = frames_dev * rows_dev * columns
    cells_all = cells_dev * lax.axis_size("frames") * lax.axis_size("rows")
    cells_clip = CLIP_FRAMES * rows_dev * lax.axis_size("rows") * columns
    group_count = channels // GROUPS * cells_clip
    grouped = act.astype(jnp.float32).reshape(GROUPS, -1)
    totals = lax.psum(picker[:, None] * jnp.sum(grouped, axis=1)[None, :], ("frames", "rows"))
    mean_table = totals / group_count
    own_mean = select_clip(mean_table, picker)
    centred = grouped - own_mean[:, None]
    variance = (
        lax.psum(picker[:, None] * jnp.sum(centred * centred, axis=1)[None, :], ("frames", "rows"))
        / group_count
    )
    rstd_table = lax.rsqrt(variance + EPS)
    group_mean = select_clip(mean_table, picker)
    group_rstd = select_clip(rstd_table, picker)
    normed, shaped = normalize(act, group_mean, group_rstd, gamma, beta)
    local_hidden = jax.nn.silu(shaped).astype(jnp.bfloat16)
    earlier = passed_along(local_hidden, "frames", 1)
    earlier = jnp.where(clip_step > 0, earlier, jnp.zeros_like(earlier))
    joined = jnp.concatenate([earlier, local_hidden], axis=1)
    activated = extended(joined, (("rows", 2),), margin)
    padded_act = jnp.pad(activated, ((0, 0), (0, 0), (0, 0), (margin, margin)))
    later = passed_along(cotangent, "frames", -1)
    later = jnp.where(clip_step < clip_span - 1, later, jnp.zeros_like(later))
    grads_ext = jnp.concatenate([cotangent, later], axis=1)
    grads_ext = extended(grads_ext, (("rows", 2),), margin)
    padded_grad = jnp.pad(grads_ext, ((0, 0), (0, 0), (0, 0), (margin, margin)))
    flat_grad = cotangent.reshape(outputs_ch, cells_dev)
    kernel_rows = []
    windows = []
    for step_t in range(KERNEL):
        for step_h in range(KERNEL):
            for step_w in range(KERNEL):
                window = padded_act[
                    :,
                    step_t : step_t + frames_dev,
                    step_h : step_h + rows_dev,
                    step_w : step_w + columns,
                ].reshape(channels, cells_dev)
                kernel_rows.append(
                    lax.dot_general(
                        window,
                        flat_grad,
                        (((1,), (1,)), ((), ())),
                        preferred_element_type=jnp.float32,
                    )
                )
                windows.append(
                    padded_grad[
                        :,
                        causal_lead - step_t : causal_lead - step_t + frames_dev,
                        2 * margin - step_h : 2 * margin - step_h + rows_dev,
                        2 * margin - step_w : 2 * margin - step_w + columns,
                    ].reshape(outputs_ch, cells_dev)
                )
    kernel_term = jnp.stack(kernel_rows).reshape(KERNEL**3, channels * outputs_ch)
    scale = float(cells_all) ** (-0.5)
    kernel_sum = lax.psum_scatter(kernel_term, ("frames", "rows"), scatter_dimension=1, tiled=True)
    stacked = jnp.stack(windows)
    hidden_grad = jnp.einsum("koi,kon->in", kernel, stacked, preferred_element_type=jnp.float32)
    sigmoid_z = jax.nn.sigmoid(shaped)
    shaped_grad = hidden_grad.reshape(shaped.shape) * sigmoid_z * (1.0 + shaped * (1.0 - sigmoid_z))
    local_gamma = jnp.sum(shaped_grad * normed, axis=(1, 2, 3))
    local_beta = jnp.sum(shaped_grad, axis=(1, 2, 3))
    gamma_clip, beta_clip = lax.psum(
        (picker[:, None] * local_gamma[None, :], picker[:, None] * local_beta[None, :]),
        ("frames", "rows"),
    )
    first_table = (
        jnp.sum((gamma[None, :] * beta_clip).reshape(clip_count, GROUPS, -1), axis=2) / group_count
    )
    second_table = (
        jnp.sum((gamma[None, :] * gamma_clip).reshape(clip_count, GROUPS, -1), axis=2) / group_count
    )
    first = select_clip(first_table, picker)
    second = select_clip(second_table, picker)
    normed_grad = (shaped_grad * gamma[:, None, None, None]).reshape(GROUPS, channels // GROUPS, -1)
    normed_group = normed.reshape(GROUPS, channels // GROUPS, -1)
    act_grad = group_rstd[:, None, None] * (
        normed_grad - first[:, None, None] - normed_group * second[:, None, None]
    )
    act_grad = act_grad.reshape(act.shape).astype(jnp.bfloat16)
    gamma_grad = jnp.sum(gamma_clip, axis=0) * scale
    beta_grad = jnp.sum(beta_clip, axis=0) * scale
    return (act_grad, kernel_sum * scale, gamma_grad, beta_grad, mean_table, rstd_table)


def solution(mesh):
    in_specs = (P(None, "frames", "rows", None), P(None, "frames", "rows", None), P(), P(), P())
    out_specs = (P(None, "frames", "rows", None), P(None, ("frames", "rows")), P(), P(), P(), P())
    return jax.shard_map(
        on_device, mesh=mesh, in_specs=in_specs, out_specs=out_specs, check_vma=False
    )
```

profile of v0, /device:TPU:1, one launch (start us, length us, event | category | flops | bytes accessed | tf_op | source)
XLA Modules:
  0.0 863.6 jit_solution(17331560932034020218)
XLA Ops:
  7.2 8.9 %collective-permute-start = (bf16[96,2,1,128]{3,1,2,0:T(2,128)(2,1)}, bf16[96,2,1,128]{3,1,2,0:T(2,128)(2,1)S(1)}, u32[]{:S(2)}, u32[]{:S(2)}) collective-permute-start(bf16[96,2,1,128]{3,1,2,0:T(2,128)(2,1)} %param.6), channel_id=1, source_target_pairs={{4,0},{8,4},{12,8},{16,12},{20,16},{24,20},{28,24},{32,28},{36,32}... | collective-permute-start | bytes 147464 | tf_op jit(solution)/shard_map/ppermute | solution.py:17
  16.2 1.1 convert_reduce_fusion
  17.6 106.4 %psum.28 = f32[16,32]{1,0:T(8,128)S(1)} all-reduce(f32[16,32]{1,0:T(8,128)S(1)} %broadcast_multiply_fusion.6), channel_id=1, replica_groups=mesh['frames'=128,'rows'=4] {'frames','rows'}, use_global_device_ids=true, to_apply=%region_2.3 | all-reduce | flops 512 | bytes 4096 | tf_op jit(solution)/shard_map/psum | solution.py:61
  124.8 1.2 fusion.27
  126.2 99.4 %psum.29 = f32[16,32]{1,0:T(8,128)S(1)} all-reduce(f32[16,32]{1,0:T(8,128)S(1)} %broadcast_multiply_fusion.5), channel_id=1, replica_groups=mesh['frames'=128,'rows'=4] {'frames','rows'}, use_global_device_ids=true, to_apply=%region_6.7 | all-reduce | flops 512 | bytes 4096 | tf_op jit(solution)/shard_map/psum | solution.py:66
  227.3 0.9 pad_maximum_fusion.1
  228.3 1.3 collective-permute-start.2
  229.6 4.0 collective-permute-start.1
  233.6 0.9 fusion.33
  235.9 1.1 fusion.64
  240.1 1.4 constant_dynamic-update-slice_fusion.25
  241.5 1.4 constant_dynamic-update-slice_fusion.24
  257.8 2.3 fusion.69
  260.4 1.1 fusion.62
  261.4 5.9 collective-permute-start.3
  267.3 2.6 collective-permute-done.3
  270.7 1.3 collective-permute-start.5
  272.0 7.7 collective-permute-start.4
  279.7 0.9 convolution_bitcast_fusion.4
  280.6 1.8 stack.110
  283.3 1.8 stack.92
  285.1 0.9 convolution_bitcast_fusion.13
  286.0 1.8 stack.101
  287.8 2.1 select_maximum_fusion
  290.8 0.9 convolution_bitcast_fusion.24
  291.7 0.9 convolution_bitcast_fusion.23
  292.6 0.9 convolution_bitcast_fusion.21
  293.5 0.9 convolution_bitcast_fusion.20
  294.4 0.9 convolution_bitcast_fusion.18
  296.2 0.9 convolution_bitcast_fusion.15
  297.1 0.9 convolution_bitcast_fusion.14
  298.0 0.9 convolution_bitcast_fusion.12
  299.8 0.9 convolution_bitcast_fusion.9
  300.7 0.9 convolution_bitcast_fusion.8
  301.6 0.9 convolution_bitcast_fusion.6
  303.4 0.9 convolution_bitcast_fusion.3
  304.8 1.8 stack.88
  307.5 1.8 stack.89
  309.3 1.8 stack.90
  311.2 1.8 stack.91
  313.0 1.8 stack.93
  314.8 1.8 stack.94
  316.6 0.9 convolution_bitcast_fusion.19
  317.5 1.8 stack.95
  319.3 1.8 stack.96
  321.2 1.8 stack.97
  323.9 1.8 stack.98
  325.7 1.8 stack.99
  327.5 1.8 stack.100
  329.3 1.8 stack.102
  331.1 1.8 stack.103
  333.8 1.8 stack.104
  335.7 1.8 stack.105
  337.5 1.8 stack.106
  340.2 1.8 stack.107
  342.0 1.9 stack.108
  343.8 1.8 stack.109
  345.6 1.8 stack.111
  347.5 0.9 stack.112
  349.1 16.8 %stack.115 = f32[27,36864]{1,0:T(8,128)} concatenate(f32[1,36864]{1,0:T(1,128)} %stack.88, f32[1,36864]{1,0:T(1,128)} %stack.89, f32[1,36864]{1,0:T(1,128)} %stack.90, f32[1,36864]{1,0:T(1,128)} %stack.91, f32[1,36864]{1,0:T(1,128)} %stack.92, f32[1,36864]{1,0:T(1,128)} %stack.93, f32[1,36864]{1,0:T(1,128)} %stack.94, f32[1,36864]{1,0:T(1,128)} %stack.95, f32[1,36864]{1,0:T(1,128)} %stack.96, ...), dimensions={0} | concatenate | bytes 7962624 | tf_op jit(solution)/shard_map/stack | solution.py:112
  366.0 109.2 %all-reduce.3 = (f32[16,384]{1,0:T(8,128)S(1)}, f32[16,384]{1,0:T(8,128)S(1)}) all-reduce(f32[16,384]{1,0:T(8,128)S(1)} %get-tuple-element.65, f32[16,384]{1,0:T(8,128)S(1)} %get-tuple-element.64), channel_id=1, replica_groups=mesh['frames'=128,'rows'=4] {'frames','rows'}, use_global_device_ids=true, to_apply=%region_9.10 | all-reduce | flops 12288 | bytes 98304 | tf_op jit(solution)/shard_map/psum | solution.py:121
  476.8 0.9 copy.154
  478.8 376.4 %all-reduce.6.cloned.1.call-done = f32[27,36864]{1,0:T(8,128)} async-done(((f32[27,36864]{1,0:T(8,128)}), f32[27,36864]{1,0:T(8,128)}) %all-reduce.6.cloned.1.call-update) | async-done | bytes 3981328
  855.3 1.4 dynamic-slice_multiply_fusion
  (122 shorter events, 35.1 us)
Async XLA Ops:
  7.2 250.7 %copy-start = (bf16[27,96,384]{2,1,0:T(8,128)(2,1)S(1)}, bf16[27,96,384]{2,1,0:T(8,128)(2,1)}, u32[]{:S(2)}) copy-start(bf16[27,96,384]{2,1,0:T(8,128)(2,1)} %param.7) | copy-start | bytes 5971972
  7.2 228.0 %copy-start.1 = (bf16[96,2,1,128]{3,1,2,0:T(2,128)(2,1)S(1)}, bf16[96,2,1,128]{3,1,2,0:T(2,128)(2,1)}, u32[]{:S(2)}) copy-start(bf16[96,2,1,128]{3,1,2,0:T(2,128)(2,1)} %param.6) | copy-start | bytes 147460
  7.2 848.1 %all-reduce.6.cloned.1.call-start = ((), (), s32[]{:S(2)}) async-start(), calls=%async_computation | async-start | bytes 9437184
  7.2 220.0 %collective-permute-start = (bf16[96,2,1,128]{3,1,2,0:T(2,128)(2,1)}, bf16[96,2,1,128]{3,1,2,0:T(2,128)(2,1)S(1)}, u32[]{:S(2)}, u32[]{:S(2)}) collective-permute-start(bf16[96,2,1,128]{3,1,2,0:T(2,128)(2,1)} %param.6), channel_id=1, source_target_pairs={{4,0},{8,4},{12,8},{16,12},{20,16},{24,20},{28,24},{32,28},{36,32}... | collective-permute-start | bytes 147464 | tf_op jit(solution)/shard_map/ppermute | solution.py:17
  228.3 6.3 collective-permute-start.2
  229.6 5.6 collective-permute-start.1
  257.8 2.5 copy-start.2
  257.8 2.5 copy-start.5
  257.8 2.5 copy-start.6
  261.4 8.5 collective-permute-start.3
  270.7 17.1 %collective-permute-start.5 = (bf16[384,4,1,128]{3,0,1,2:T(8,128)(2,1)}, bf16[384,4,1,128]{3,0,1,2:T(8,128)(2,1)S(1)}, u32[]{:S(2)}, u32[]{:S(2)}) collective-permute-start(bf16[384,4,1,128]{3,0,1,2:T(8,128)(2,1)} %pad_maximum_fusion), channel_id=1, source_target_pairs={{1,0},{2,1},{3,2},{5,4},{6,5},{7,6},{9,8},{10,9},{11,10},{13,12},{... | collective-permute-start | bytes 1179656 | tf_op jit(solution)/shard_map/ppermute | solution.py:28
  272.0 15.8 %collective-permute-start.4 = (bf16[384,4,1,128]{3,0,1,2:T(8,128)(2,1)}, bf16[384,4,1,128]{3,0,1,2:T(8,128)(2,1)S(1)}, u32[]{:S(2)}, u32[]{:S(2)}) collective-permute-start(bf16[384,4,1,128]{3,0,1,2:T(8,128)(2,1)} %pad_maximum_fusion), channel_id=1, source_target_pairs={{0,1},{1,2},{2,3},{4,5},{5,6},{6,7},{8,9},{9,10},{10,11},{12,13},{... | collective-permute-start | bytes 1179656 | tf_op jit(solution)/shard_map/ppermute | solution.py:25
  342.0 7.1 copy-start.4
  365.9 110.6 %copy-start.3 = (f32[384,2,1,128]{3,0,1,2:T(8,128)S(1)}, f32[384,2,1,128]{3,0,1,2:T(8,128)}, u32[]{:S(2)}) copy-start(f32[384,2,1,128]{3,0,1,2:T(8,128)} %get-tuple-element.30) | copy-start | bytes 1179652
Sparse Core Ops, SparseCore 0:
  366.0 489.2 all-reduce.5
where the time goes:
time: 867 us; the launch traced here: 864 us
  waiting for transfers between devices  380 us (44%)
  blocking collectives  315 us (36%)
  local copies, waits for them, and re-layouts  87.1 us (10%)
  starting transfers between devices  29.1 us (3%)
  matrix products  24.4 us (3%)
  between operations  14.6 us (2%)
  other arithmetic  13.8 us (2%)
    unnamed x2, waiting for transfers between devices  376 us
    psum x1, blocking collectives, on_device(): lax.psum((picker[:, None] * local_gamma[None, :], picker[:, None] * local...  109 us
    psum x1, blocking collectives, on_device(): lax.psum(picker[:, None] * jnp.sum(grouped, axis=1)[None, :], ('frames',...  106 us
    psum x1, blocking collectives, on_device(): lax.psum(picker[:, None] * jnp.sum(centred * centred, axis=1)[None, :], (...  99.4 us
    another operation x28, local copies, waits for them, and re-layouts, on_device(): jnp.stack(kernel_rows).reshape(KERNEL ** 3, channels * outputs_ch)  61.9 us
    dot_general x27, matrix products, on_device(): lax.dot_general(window, flat_grad, (((1,), (1,)), ((), ())), preferred_el...  22.1 us
    unnamed x41, local copies, waits for them, and re-layouts  18.6 us
  transfers between devices with their start and end apart: 7, of which 3 were waited for; matrix products, arithmetic and copies ran while one was open for 2% of the time, Pallas kernels for 0%

commit v1 on v0

v1 whole, which is shorter than its diff:
```python
import functools

import jax
import jax.numpy as jnp
from jax import lax
from jax.experimental import pallas as pl
from jax.experimental.pallas import tpu as pltpu
from jax.sharding import PartitionSpec as P

GROUPS = 32
KERNEL = 3
LANES = 128
EPS = 1e-06
F32 = jnp.float32
BF16 = jnp.bfloat16
MESH = pl.DeviceIdType.MESH


def remote(src, dst, send_sem, recv_sem, device):
    return pltpu.make_async_remote_copy(
        src_ref=src,
        dst_ref=dst,
        send_sem=send_sem,
        recv_sem=recv_sem,
        device_id=device,
        device_id_type=MESH,
    )


def others(count, me, step, farthest=False):
    def body(d, carry):
        if farthest:
            d = count // 2 + (d // 2) * (1 - 2 * lax.rem(d, 2))
        step(lax.rem(me + d, count))
        return carry

    lax.fori_loop(1, count, body, 0)


def exchange(buf, send, recv, count, me, device):
    def copy(slot, peer):
        return remote(buf.at[slot], buf.at[slot], send.at[peer], recv.at[slot], device(peer))

    return (
        lambda: others(count, me, lambda p: copy(me, p).start(), True),
        lambda: others(count, me, lambda p: copy(p, p).wait_recv()),
        lambda: others(count, me, lambda p: copy(me, p).wait_send()),
    )


def listed(buf):
    return jnp.concatenate([buf[n] for n in range(buf.shape[0])], axis=0)


def body(
    sizes,
    act_ref,
    cot_ref,
    kernel_ref,
    gamma_ref,
    beta_ref,
    act_grad_ref,
    kernel_grad_ref,
    gamma_grad_ref,
    beta_grad_ref,
    mean_ref,
    rstd_ref,
    act_raw,
    cot_raw,
    gamma_raw,
    beta_raw,
    act_grad,
    kernel_grad,
    gamma_grad,
    beta_grad,
    mean_table,
    rstd_table,
    x_ref,
    stats,
    ring,
    groups,
    affine,
    affine_all,
    blocks,
    slabs,
    weights,
    perm,
    mask_a,
    mask_b,
    gain,
    own_mask,
    own_gain,
    normed_ref,
    slope_ref,
    grad_ref,
    act_out,
    act_in,
    partial,
    by_owner,
    plane_out,
    plane_in,
    column_out,
    column_in,
    load_sem,
    store_sem,
    stats_s,
    stats_r,
    ring_s,
    ring_r,
    groups_s,
    groups_r,
    affine_s,
    affine_r,
    all_s,
    all_r,
    line_s,
    mate_s,
    next_s,
    next_line_s,
    pass_s,
    blocks_r,
    act_s,
    act_r,
    plane_s,
    plane_r,
    column_s,
    column_r,
):
    Z, YX, C, O, group_count, scale = sizes
    per_group = C // GROUPS
    half = act_raw.shape[2]
    cells = 2 * half
    width = 3 * YX
    column = 2 * Z * Z
    padded = affine_all.shape[2] // 2
    f = lax.axis_index("frames")
    zl = lax.axis_index("rows")
    core = lax.rem(f, 2)
    zh = lax.rem(f // 2, Z)
    yx = f // (2 * Z)
    rank = lax.rem(f, 2 * Z) * Z + zl
    member = core * Z + zl

    def in_column(p):
        return (yx * (2 * Z) + p // Z, lax.rem(p, Z))

    def in_plane(p):
        return (p * (2 * Z) + lax.rem(f, 2 * Z), zl)

    def in_block(p):
        return (yx * (2 * Z) + zh * 2 + p // Z, lax.rem(p, Z))

    mate = (f + 1 - 2 * core, zl)

    def across_blocks(step):
        return (yx * (2 * Z) + lax.rem(zh + step + Z, Z) * 2 + core, zl)

    partner = (yx * (2 * Z) + lax.rem(zh + 2 * core - 1 + Z, Z) * 2 + 1 - core, zl)
    steps = [Z // 2] + [step for n in range(1, Z // 2) for step in (n, -n)]

    barrier = pltpu.get_barrier_semaphore()

    def greet(device):
        pl.semaphore_signal(barrier, inc=1, device_id=device, device_id_type=MESH)

    for step in steps:
        greet(across_blocks(step))
    greet(partner)
    others(YX, yx, lambda p: greet(in_plane(p)), True)
    others(2 * Z, member, lambda p: greet(in_block(p)))

    loads = [
        pltpu.make_async_copy(source, target, load_sem.at[n])
        for n, (source, target) in enumerate(
            (
                (act_ref, act_raw),
                (cot_ref, cot_raw),
                (gamma_ref, gamma_raw),
                (beta_ref, beta_raw),
                (kernel_ref, weights.at[:, pl.ds(0, O), :]),
            )
        )
    ]
    for load in loads:
        load.start()

    chan = lax.broadcasted_iota(jnp.int32, (C, LANES), 0)
    lane = lax.broadcasted_iota(jnp.int32, (C, LANES), 1)
    first_chan = lane * per_group
    mask_a[...] = jnp.where((chan >= first_chan) & (chan < first_chan + per_group), 1.0, 0.0).astype(F32)
    place = lax.broadcasted_iota(jnp.int32, (YX, C), 0) * (6 * Z)
    source = lax.broadcasted_iota(jnp.int32, (YX, C), 1)
    for p in range(2 * Z):
        for c in range(3):
            base = p * width + c * YX
            offset = (p % Z) * 6 + (p // Z) * 3 + c
            perm[base : base + YX, :] = jnp.where(source == place + offset, 1.0, 0.0).astype(BF16)

    loads[0].wait()
    x_a = act_raw[:, 0, :].astype(F32)
    x_b = act_raw[:, 1, :].astype(F32)
    x_ref[:, :half] = x_a
    x_ref[:, half:] = x_b
    mean = jnp.sum(x_a + x_b, axis=1, keepdims=True) / cells
    squares = jnp.sum((x_a - mean) * (x_a - mean) + (x_b - mean) * (x_b - mean), axis=1, keepdims=True)
    mean_row = jnp.sum(mask_a[...] * mean, axis=0, keepdims=True) / per_group
    gap = mean - jnp.sum(mask_a[...] * mean_row, axis=1, keepdims=True)
    squares = squares + cells * (gap * gap)
    stats[member] = mean_row + pltpu.roll(jnp.sum(mask_a[...] * squares, axis=0, keepdims=True), GROUPS, 1)

    loads[1].wait()
    for side in range(2):
        blocks[core, zl, :, side * half : (side + 1) * half] = cot_raw[:, side, :].astype(F32).astype(BF16)

    ordered = jnp.dot(perm[...], x_ref[...].astype(BF16), preferred_element_type=F32).astype(BF16)
    act_out[...] = ordered.reshape(act_out.shape)
    act_in[member] = act_out[member]

    pl.semaphore_wait(barrier, len(steps) + 1 + YX - 1 + 2 * Z - 1)

    def block_copy(pair, row, send, device):
        ref = blocks.at[pair, row]
        return remote(ref, ref, send, blocks_r.at[pair, row], device)

    side_rows = Z // 2
    own_half = zl // side_rows
    gateway = side_rows - own_half
    is_gateway = zl == side_rows - 1 + own_half

    def half_peers(step):
        others(side_rows, lax.rem(zl, side_rows), lambda n: step(own_half * side_rows + n))

    def to_line(pair, sems, act):
        half_peers(lambda p: act(block_copy(pair, zl, sems.at[p], (f, p))))
        act(block_copy(pair, zl, sems.at[gateway], (f, gateway)))

    def to_mate(pair, row, which):
        return block_copy(pair, row, mate_s.at[which, row], mate)

    def landed(pair, row):
        block_copy(pair, row, line_s.at[0], mate).wait_recv()

    def start(copy):
        copy.start()

    def wait_send(copy):
        copy.wait_send()

    def passed(pair, which, act):
        @pl.when(is_gateway)
        def _():
            def across(n, carry):
                row = (1 - own_half) * side_rows + n
                half_peers(lambda p: act(block_copy(pair, row, pass_s.at[which, row], (f, p))))
                return carry

            lax.fori_loop(0, side_rows, across, 0)

    def take_line(pair, which):
        def across(n, carry):
            row = (1 - own_half) * side_rows + n
            landed(pair, row)

            @pl.when(is_gateway)
            def _():
                half_peers(lambda p: block_copy(pair, row, pass_s.at[which, row], (f, p)).start())

            to_mate(pair, row, which).start()
            return carry

        def near():
            def step(p):
                landed(pair, p)
                to_mate(pair, p, which).start()

            half_peers(step)

        def far():
            lax.fori_loop(0, side_rows, across, 0)

        near()
        far()

    gives_next = (core == 0) & (zh > 0)
    takes_next = (core == 1) & (zh < Z - 1)
    earlier = (lax.max(f - 1, 0), zl)

    def block_copy_next():
        return remote(blocks.at[core, zl], blocks.at[2, zl], next_s.at[0], blocks_r.at[2, zl], earlier)

    @pl.when(gives_next)
    def _():
        block_copy_next().start()

    start_stats, recv_stats, sent_stats = exchange(stats, stats_s, stats_r, 2 * Z, member, in_block)
    start_stats()
    to_line(core, line_s, start)
    to_mate(core, zl, 0).start()

    def act_copy(peer, slot):
        return remote(act_out.at[peer], act_in.at[slot], act_s.at[peer], act_r.at[slot], in_block(peer))

    others(2 * Z, member, lambda p: act_copy(p, member).start())

    first_chan = (lane - GROUPS) * per_group
    mask_b[...] = jnp.where((chan >= first_chan) & (chan < first_chan + per_group), 1.0, 0.0).astype(F32)
    loads[2].wait()
    loads[3].wait()
    gamma_row = gamma_raw[...].reshape(1, C)
    beta_row = beta_raw[...].reshape(1, C)
    gain[0] = jnp.broadcast_to(gamma_row, (LANES, C)).T
    gain[1] = jnp.broadcast_to(beta_row, (LANES, C)).T
    own_chan = lax.broadcasted_iota(jnp.int32, (YX, LANES), 0) * (6 * Z)
    own_lane = lax.broadcasted_iota(jnp.int32, (YX, LANES), 1) * per_group
    for c in range(3):
        at = pl.ds(c * YX, YX)
        offset = zl * 6 + core * 3 + c
        chosen = jnp.where(source == place + offset, 1.0, 0.0).astype(F32)
        own_gain[0, at, :] = jnp.broadcast_to(jnp.sum(chosen * gamma_row, axis=1, keepdims=True), (YX, LANES))
        own_gain[1, at, :] = jnp.broadcast_to(jnp.sum(chosen * beta_row, axis=1, keepdims=True), (YX, LANES))
        inside = (own_chan + offset >= own_lane) & (own_chan + offset < own_lane + per_group)
        own_mask[at, :] = jnp.where(inside, 1.0, 0.0).astype(F32)

    if O < LANES:
        weights[:, O:, :] = jnp.zeros((KERNEL**3, LANES - O, C), BF16)

    @pl.when(zh == Z - 1)
    def _():
        blocks[2] = jnp.zeros(blocks.shape[1:], BF16)

    slabs[:, 0] = jnp.zeros((5,) + slabs.shape[2:], BF16)
    slabs[:, Z + 1] = jnp.zeros((5,) + slabs.shape[2:], BF16)
    if O < LANES:
        for k in range(KERNEL):
            slabs[:, 1 : Z + 1, k * LANES + O : (k + 1) * LANES, :] = jnp.zeros((5, Z, LANES - O, cells), BF16)

    lane_row = lax.broadcasted_iota(jnp.int32, (1, LANES), 1)

    def combined(rows, cells_of_one):
        total = jnp.sum(rows, axis=0, keepdims=True)
        mean_row = jnp.where(lane_row < GROUPS, total / rows.shape[0], 0.0)
        gaps = jnp.where(lane_row < GROUPS, rows - mean_row, 0.0)
        return mean_row, pltpu.roll(total, LANES - GROUPS, 1) + cells_of_one * jnp.sum(gaps * gaps, axis=0, keepdims=True)

    recv_stats()
    block_mean, block_squares = combined(listed(stats), per_group * cells)
    ring[zh] = block_mean + pltpu.roll(jnp.where(lane_row < GROUPS, block_squares, 0.0), GROUPS, 1)

    def ring_copy(slot, which, step):
        return remote(ring.at[slot], ring.at[slot], ring_s.at[which], ring_r.at[slot], across_blocks(step))

    def block_at(step):
        return lax.rem(zh + step + Z, Z)

    for which, step in enumerate(steps):
        ring_copy(zh, which, step).start()

    take_line(core, 0)

    @pl.when(takes_next)
    def _():
        landed(2, zl)
        others(Z, zl, lambda p: block_copy(2, zl, next_line_s.at[p], (f, p)).start())
        to_mate(2, zl, 1).start()

    def from_mate(row, carry):
        landed(1 - core, row)
        return carry

    lax.fori_loop(0, Z, from_mate, 0)

    column_lane = lax.broadcasted_iota(jnp.int32, (O, half), 1)

    def fill(frames):
        def fill_row(row, carry):
            for frame in frames:
                slab = blocks[frame // 2, row, :, (frame % 2) * half : (frame % 2 + 1) * half]
                wide = slab.astype(F32)
                shifted = (
                    jnp.where(column_lane < half - 1, pltpu.roll(wide, half - 1, 1), 0.0).astype(BF16),
                    slab,
                    jnp.where(column_lane > 0, pltpu.roll(wide, 1, 1), 0.0).astype(BF16),
                )
                for k in range(KERNEL):
                    if frame < 5:
                        slabs[frame, row + 1, k * LANES : k * LANES + O, :half] = shifted[k]
                    if frame > 0:
                        slabs[frame - 1, row + 1, k * LANES : k * LANES + O, half:] = shifted[k]
            return carry

        lax.fori_loop(0, Z, fill_row, 0)

    fill(range(4))

    def gradient(lags):
        total = grad_ref[...]
        for i in lags:
            for j in range(KERNEL):
                tap = (i * KERNEL + j) * KERNEL
                total += lax.dot_general(
                    weights[tap : tap + KERNEL].reshape(KERNEL * LANES, C),
                    slabs[2 * core + 2 - i, zl - j + 2],
                    (((0,), (0,)), ((), ())),
                    preferred_element_type=F32,
                )
        grad_ref[...] = total

    loads[4].wait()
    grad_ref[...] = jnp.zeros((C, cells), F32)
    gradient((2,))


    for step in steps:
        ring_copy(block_at(step), 0, step).wait_recv()
    mean_row, squares_row = combined(listed(ring), 2 * Z * per_group * cells)
    rstd_row = jnp.where(
        lane_row < GROUPS, lax.rsqrt(jnp.where(lane_row < GROUPS, squares_row, 0.0) / group_count + EPS), 0.0
    )
    affine[yx, :, 2 * padded :] = jnp.where(
        lane_row < GROUPS, mean_row, jnp.where(lane_row < 2 * GROUPS, pltpu.roll(rstd_row, GROUPS, 1), 0.0)
    )

    others(2 * Z, member, lambda p: act_copy(member, p).wait_recv())

    own_mean = jnp.sum(own_mask[...] * mean_row, axis=1, keepdims=True)
    own_rstd = jnp.sum(own_mask[...] * rstd_row, axis=1, keepdims=True)
    own_gamma, own_beta = own_gain[0, :, :1], own_gain[1, :, :1]
    for slot in range(2 * Z):
        shaped = (act_in[slot].astype(F32) - own_mean) * own_rstd * own_gamma + own_beta
        act_in[slot] = (shaped / (1.0 + jnp.exp(-shaped))).astype(BF16)

    partial[...] = jnp.zeros(partial.shape, F32)

    def correlate(lead):
        for row in range(Z):
            low, high = max(0, row - 1), min(Z - 1, row + 1)
            count = high - low + 1
            for side in range(2):
                i = 2 * side + 2 - lead
                if not 0 <= i < KERNEL:
                    continue
                product = lax.dot_general(
                    act_in[side * Z + low : side * Z + high + 1].reshape(count * width, cells),
                    slabs[lead, row + 1],
                    (((1,), (1,)), ((), ())),
                    preferred_element_type=F32,
                )
                for n in range(count):
                    j = low + n + 1 - row
                    partial[i * KERNEL + j] += product[n * width : (n + 1) * width]

    @pl.when(takes_next)
    def _():
        def pass_next(row):
            landed(2, row)
            to_mate(2, row, 1).start()

        others(Z, zl, pass_next)

    for lead in range(3):
        correlate(lead)

    mean = jnp.sum(mask_a[...] * mean_row, axis=1, keepdims=True)
    rstd = jnp.sum(mask_a[...] * rstd_row, axis=1, keepdims=True)
    for side in range(2):
        at = pl.ds(side * half, half)
        normed = (x_ref[:, at] - mean) * rstd
        shaped = normed * gain[0] + gain[1]
        sig = 1.0 / (1.0 + jnp.exp(-shaped))
        normed_ref[:, at] = normed
        slope_ref[:, at] = sig * (1.0 + shaped * (1.0 - sig))

    @pl.when((core == 0) & (zh < Z - 1))
    def _():
        def next_from_mate(row, carry):
            landed(2, row)
            return carry

        lax.fori_loop(0, Z, next_from_mate, 0)

    fill(range(4, 6))

    gradient((0, 1))
    shaped_grad = grad_ref[...] * slope_ref[...]
    slope_ref[...] = shaped_grad
    scaled = shaped_grad * normed_ref[...]
    beta_sum = jnp.sum(shaped_grad[:, :half] + shaped_grad[:, half:], axis=1, keepdims=True)
    gamma_sum = jnp.sum(scaled[:, :half] + scaled[:, half:], axis=1, keepdims=True)
    affine[yx, :, 0:C] = jnp.broadcast_to(gamma_sum, (C, LANES)).T[:1]
    affine[yx, :, padded : padded + C] = jnp.broadcast_to(beta_sum, (C, LANES)).T[:1]
    start_affine, recv_affine, sent_affine = exchange(affine, affine_s, affine_r, YX, yx, in_plane)
    start_affine()
    groups[rank] = jnp.sum(
        gain[0] * (mask_a[...] * beta_sum + mask_b[...] * gamma_sum), axis=0, keepdims=True
    )
    for lead in range(3, 5):
        correlate(lead)

    by_owner[...] = jnp.zeros(by_owner.shape, F32)

    tile_rows = min(8, YX)
    tiles = YX // tile_rows

    def arrange(tile, carry):
        c = tile // tiles
        first_place = lax.rem(tile, tiles) * tile_rows
        at = pl.ds(pl.multiple_of(tile * tile_rows, tile_rows), tile_rows)
        for ij in range(KERNEL**2):
            for k in range(KERNEL):
                tap = ij * KERNEL + k
                values = partial[ij, at, k * LANES : (k + 1) * LANES]
                for row in range(tile_rows):
                    by_owner[(first_place + row) * 3 + c, tap : tap + 1, :] = values[row : row + 1]
        return carry

    lax.fori_loop(0, 3 * tiles, arrange, 0)
    plane_out[...] = by_owner[...].astype(BF16).reshape(plane_out.shape)

    def plane_copy(peer, slot):
        return remote(plane_out.at[peer], plane_in.at[slot], plane_s.at[peer], plane_r.at[slot], in_plane(peer))

    others(YX, yx, lambda p: plane_copy(p, yx).start())
    plane_in[yx] = jnp.zeros(plane_in.shape[1:], BF16)

    start_groups, recv_groups, sent_groups = exchange(groups, groups_s, groups_r, column, rank, in_column)
    start_groups()

    recv_affine()
    affine_rows = listed(affine)
    mean_table[...] = affine_rows[:, 2 * padded : 2 * padded + GROUPS]
    rstd_table[...] = affine_rows[:, 2 * padded + GROUPS : 2 * padded + 2 * GROUPS]
    stores = [
        pltpu.make_async_copy(source, target, store_sem.at[n])
        for n, (source, target) in enumerate(
            (
                (mean_table, mean_ref),
                (rstd_table, rstd_ref),
                (act_grad, act_grad_ref),
                (gamma_grad, gamma_grad_ref),
                (beta_grad, beta_grad_ref),
                (kernel_grad, kernel_grad_ref),
            )
        )
    ]
    stores[0].start()
    stores[1].start()
    affine_all[rank] = jnp.sum(affine_rows[:, : 2 * padded], axis=0, keepdims=True)
    start_all, recv_all, sent_all = exchange(affine_all, all_s, all_r, column, rank, in_column)
    start_all()

    others(YX, yx, lambda p: plane_copy(yx, p).wait_recv())

    def add(slot, carry):
        return carry + plane_in[slot].astype(F32)

    summed = lax.fori_loop(0, YX, add, by_owner[pl.ds(3 * yx, 3)])
    share = 3 * O // Z
    tap_lane = lax.broadcasted_iota(jnp.int32, summed.shape[1:], 1)
    for part in range(Z):
        packed = jnp.zeros(summed.shape[1:], F32)
        for c in range(3):
            low, high = max(share * part, O * c), min(share * (part + 1), O * (c + 1))
            if high <= low:
                continue
            inside = (tap_lane >= low - share * part) & (tap_lane < high - share * part)
            shift = (O * c - share * part) % LANES
            moved = pltpu.roll(summed[c], shift, 1) if shift else summed[c]
            packed = jnp.where(inside, moved, packed)
        column_out[part] = packed

    def column_copy(part, slot):
        device = (yx * (2 * Z) + zl * 2 + core, part)
        return remote(column_out.at[part], column_in.at[slot], column_s.at[part], column_r.at[slot], device)

    at_home = zh == zl

    def send_part(part, carry):
        stays = at_home & (part == zl)

        @pl.when(jnp.logical_not(stays))
        def _():
            column_copy(part, zh).start()

        @pl.when(stays)
        def _():
            column_in[zh] = column_out[part]

        return carry

    lax.fori_loop(0, Z, send_part, 0)

    recv_groups()
    group_row = jnp.sum(listed(groups), axis=0, keepdims=True) / group_count
    first = jnp.sum(mask_a[...] * group_row, axis=1, keepdims=True)
    second = jnp.sum(mask_b[...] * group_row, axis=1, keepdims=True)
    for side in range(2):
        at = pl.ds(side * half, half)
        act_grad[:, side, :] = (
            rstd * (gain[0] * slope_ref[:, at] - first - normed_ref[:, at] * second)
        ).astype(BF16)
    stores[2].start()

    recv_all()
    totals = jnp.sum(listed(affine_all), axis=0, keepdims=True) * scale
    gamma_grad[...] = totals[:, :C].reshape(C)
    beta_grad[...] = totals[:, padded : padded + C].reshape(C)
    stores[3].start()
    stores[4].start()

    sent_stats()
    for which, step in enumerate(steps):
        ring_copy(zh, which, step).wait_send()
    sent_groups()
    sent_affine()
    sent_all()

    @pl.when(gives_next)
    def _():
        block_copy_next().wait_send()

    to_line(core, line_s, wait_send)
    passed(core, 0, wait_send)

    def mate_sent(row, carry):
        to_mate(core, row, 0).wait_send()
        return carry

    lax.fori_loop(0, Z, mate_sent, 0)

    @pl.when(takes_next)
    def _():
        others(Z, zl, lambda p: block_copy(2, zl, next_line_s.at[p], (f, p)).wait_send())

        def next_sent(row, carry):
            to_mate(2, row, 1).wait_send()
            return carry

        lax.fori_loop(0, Z, next_sent, 0)

    others(2 * Z, member, lambda p: act_copy(p, member).wait_send())
    others(YX, yx, lambda p: plane_copy(p, yx).wait_send())

    def take_part(slot, carry):
        @pl.when(jnp.logical_not(at_home & (slot == zh)))
        def _():
            column_copy(0, slot).wait_recv()

        return carry

    lax.fori_loop(0, Z, take_part, 0)
    result = jnp.sum(column_in[...], axis=0) * scale
    kernel_grad[...] = result[: KERNEL**3, :share]
    stores[5].start()

    def part_sent(part, carry):
        @pl.when(jnp.logical_not(at_home & (part == zl)))
        def _():
            column_copy(part, zh).wait_send()

        return carry

    lax.fori_loop(0, Z, part_sent, 0)
    for store in stores:
        store.wait()


def hand_over(*refs):
    count = len(refs) // 3
    sources, targets, holds = refs[:count], refs[count : 2 * count], refs[2 * count : 3 * count]
    load_sem, store_sem = refs[3 * count :]
    loads = [pltpu.make_async_copy(sources[n], holds[n], load_sem.at[n]) for n in range(count)]
    stores = [pltpu.make_async_copy(holds[n], targets[n], store_sem.at[n]) for n in range(count)]
    for load in loads:
        load.start()
    for load, store in zip(loads, stores):
        load.wait()
        store.start()
    for store in stores:
        store.wait()


def on_device(Z, YX, act, cotangent, kernel, gamma, beta):
    C, frames, rows, half = act.shape
    O = cotangent.shape[0]
    cells = frames * rows * half
    column = 2 * Z * Z
    group_count = C // GROUPS * cells * column
    scale = float(cells * column * YX) ** (-0.5)
    padded = -(-C // LANES) * LANES
    sizes = (Z, YX, C, O, group_count, scale)
    hbm = pl.BlockSpec(memory_space=pl.ANY)
    dma = pltpu.SemaphoreType.DMA
    width = 3 * YX
    outputs = (
        jax.ShapeDtypeStruct((C, frames, half), BF16),
        jax.ShapeDtypeStruct((KERNEL**3, 3 * O // Z), F32),
        jax.ShapeDtypeStruct((C,), F32),
        jax.ShapeDtypeStruct((C,), F32),
        jax.ShapeDtypeStruct((YX, GROUPS), F32),
        jax.ShapeDtypeStruct((YX, GROUPS), F32),
    )
    scratch = [
        pltpu.VMEM((C, frames, half), BF16),
        pltpu.VMEM((O, frames, half), BF16),
        pltpu.VMEM((C,), F32),
        pltpu.VMEM((C,), F32),
        *(pltpu.VMEM(out.shape, out.dtype) for out in outputs),
        pltpu.VMEM((C, cells), F32),
        pltpu.VMEM((2 * Z, 1, LANES), F32),
        pltpu.VMEM((Z, 1, LANES), F32),
        pltpu.VMEM((column, 1, LANES), F32),
        pltpu.VMEM((YX, 1, 2 * padded + LANES), F32),
        pltpu.VMEM((column, 1, 2 * padded), F32),
        pltpu.VMEM((3, Z, O, cells), BF16),
        pltpu.VMEM((5, Z + 2, KERNEL * LANES, cells), BF16),
        pltpu.VMEM((KERNEL**3, LANES, C), BF16),
        pltpu.VMEM((C, C), BF16),
        pltpu.VMEM((C, LANES), F32),
        pltpu.VMEM((C, LANES), F32),
        pltpu.VMEM((2, C, LANES), F32),
        pltpu.VMEM((width, LANES), F32),
        pltpu.VMEM((2, width, LANES), F32),
        pltpu.VMEM((C, cells), F32),
        pltpu.VMEM((C, cells), F32),
        pltpu.VMEM((C, cells), F32),
        pltpu.VMEM((2 * Z, width, cells), BF16),
        pltpu.VMEM((2 * Z, width, cells), BF16),
        pltpu.VMEM((KERNEL**2, width, KERNEL * LANES), F32),
        pltpu.VMEM((width, 32, LANES), F32),
        pltpu.VMEM((YX, 3, 32, LANES), BF16),
        pltpu.VMEM((YX, 3, 32, LANES), BF16),
        pltpu.VMEM((Z, 32, LANES), F32),
        pltpu.VMEM((Z, 32, LANES), F32),
        dma((5,)),
        dma((6,)),
        dma((2 * Z,)),
        dma((2 * Z,)),
        dma((3,)),
        dma((Z,)),
        dma((column,)),
        dma((column,)),
        dma((YX,)),
        dma((YX,)),
        dma((column,)),
        dma((column,)),
        dma((Z,)),
        dma((2, Z)),
        dma((1,)),
        dma((Z,)),
        dma((2, Z)),
        dma((3, Z)),
        dma((2 * Z,)),
        dma((2 * Z,)),
        dma((YX,)),
        dma((YX,)),
        dma((Z,)),
        dma((Z,)),
    ]
    results = pl.pallas_call(
        functools.partial(body, sizes),
        out_shape=outputs,
        in_specs=[hbm] * 5,
        out_specs=(hbm,) * 6,
        scratch_shapes=scratch,
        compiler_params=pltpu.CompilerParams(
            collective_id=0, has_side_effects=True, vmem_limit_bytes=62 * 2**20
        ),
        name="unit_backward",
    )(
        act.reshape(C, frames, half),
        cotangent.reshape(O, frames, half),
        kernel,
        gamma,
        beta,
    )
    results = pl.pallas_call(
        hand_over,
        out_shape=outputs,
        in_specs=[hbm] * 6,
        out_specs=(hbm,) * 6,
        scratch_shapes=[*(pltpu.VMEM(out.shape, out.dtype) for out in outputs), dma((6,)), dma((6,))],
        name="hand_over",
    )(*results)
    return (results[0].reshape(act.shape), *results[1:])


def solution(mesh):
    Z = mesh.shape["rows"]
    YX = mesh.shape["frames"] // (2 * Z)
    in_specs = (P(None, "frames", "rows", None), P(None, "frames", "rows", None), P(), P(), P())
    out_specs = (P(None, "frames", "rows", None), P(None, ("frames", "rows")), P(), P(), P(), P())
    return jax.shard_map(
        functools.partial(on_device, Z, YX), mesh=mesh, in_specs=in_specs, out_specs=out_specs, check_vma=False
    )
```

time: 867 us -> 55.7 us (0.06)
  waiting for transfers between devices: 380 us -> 0 us
  blocking collectives: 315 us -> 0 us
  local copies, waits for them, and re-layouts: 87.1 us -> 0 us
  Pallas kernels: 0 us -> 54.9 us
  starting transfers between devices: 29.1 us -> 0 us
  matrix products: 24.4 us -> 0 us
  between operations: 14.6 us -> 0.64 us
  other arithmetic: 13.8 us -> 0 us
    unnamed x2 -> x0, waiting for transfers between devices: 376 us -> none
    psum x3 -> x0, blocking collectives: 315 us -> none  [the longest x1 109 us: on_device(): lax.psum((picker[:, None] * local_gamma[None, :], picker[:, None] * local...]
    another operation x56 -> x0, local copies, waits for them, and re-layouts: 65.6 us -> none  [the longest x28 61.9 us: on_device(): jnp.stack(kernel_rows).reshape(KERNEL ** 3, channels * outputs_ch)]
    pallas_call x0 -> x2, Pallas kernels: none -> 54.9 us  [the longest x1 53.1 us: on_device(): pl.pallas_call(functools.partial(body, sizes), out_shape=outputs, in_spec...]
    ppermute x6 -> x0, starting transfers between devices: 29 us -> none  [the longest x2 14.8 us: passed_along(): return lax.ppermute(array, axis, pairs)]
    dot_general x28 -> x0, matrix products: 24.4 us -> none  [the longest x27 22.1 us: on_device(): lax.dot_general(window, flat_grad, (((1,), (1,)), ((), ())), preferred_el...]
    unnamed x41 -> x0, local copies, waits for them, and re-layouts: 18.6 us -> none
  transfers between devices with their start and end apart: 7 -> 0, of which waited for: 3 -> 0; matrix products, arithmetic and copies ran while one was open for 2% -> 0% of each run, Pallas kernels for 0% -> 0%
where the time goes in v1:
time: 55.7 us; the launch traced here: 55.5 us
  Pallas kernels  54.9 us (99%)
  between operations  0.64 us (1%)
    pallas_call x1, Pallas kernels, on_device(): pl.pallas_call(functools.partial(body, sizes), out_shape=outputs, in_spec...  53.1 us
    pallas_call x1, Pallas kernels, on_device(): pl.pallas_call(hand_over, out_shape=outputs, in_specs=[hbm] * 6, out_spec...  1.72 us

profile of v1, /device:TPU:1, one launch (start us, length us, event | category | flops | bytes accessed | tf_op | source)
XLA Modules:
  0.0 55.5 jit_solution(15925570405650941139)
XLA Ops:
  0.6 53.1 %unit_backward.1 = (bf16[384,2,128]{2,1,0:T(2,128)(2,1)}, f32[27,72]{1,0:T(8,128)}, f32[384]{0:T(512)}, f32[384]{0:T(512)}, f32[16,32]{1,0:T(8,128)}, /*index=5*/f32[16,32]{1,0:T(8,128)}) custom-call(bf16[384,2,128]{2,1,0:T(2,128)(2,1)} %bitcast.5, bf16[96,2,128]{2,1,0:T(2,128)(2,1)} %bitcast.6, bf16[27,96,384]{2,1,0:T(8,128)(2,1)} %kernel_ref.1, ...), custom_call_target="tpu_custom_call" | custom-call | tf_op jit(solution)/shard_map/unit_backward/pallas_call | solution.py:759
  53.8 1.7 %hand_over.1 = (bf16[384,2,128]{2,1,0:T(2,128)(2,1)}, f32[27,72]{1,0:T(8,128)}, f32[384]{0:T(512)}, f32[384]{0:T(512)}, f32[16,32]{1,0:T(8,128)}, /*index=5*/f32[16,32]{1,0:T(8,128)}) custom-call(bf16[384,2,128]{2,1,0:T(2,128)(2,1)} %get-tuple-element.18.refs_0_, f32[27,72]{1,0:T(8,128)} %get-tuple-element.19.refs_1_, f32[384]{0:T(512)} %get-tuple-element.20.refs_2_, ...), custom_call_target="tpu_custom_call" | custom-call | tf_op jit(solution)/shard_map/hand_over/pallas_call | solution.py:776

commit v2 on v1

--- a/solution.py
+++ b/solution.py
@@ -78,9 +78,9 @@
     x_ref,
     stats,
     ring,
-    groups,
+    sums,
+    clip_sums,
     affine,
-    affine_all,
     blocks,
     slabs,
     weights,
@@ -107,12 +107,12 @@
     stats_r,
     ring_s,
     ring_r,
-    groups_s,
-    groups_r,
+    sums_s,
+    sums_r,
+    clip_sums_s,
+    clip_sums_r,
     affine_s,
     affine_r,
-    all_s,
-    all_r,
     line_s,
     mate_s,
     next_s,
@@ -131,18 +131,13 @@
     half = act_raw.shape[2]
     cells = 2 * half
     width = 3 * YX
-    column = 2 * Z * Z
-    padded = affine_all.shape[2] // 2
+    padded = (affine.shape[2] - LANES) // 2
     f = lax.axis_index("frames")
     zl = lax.axis_index("rows")
     core = lax.rem(f, 2)
     zh = lax.rem(f // 2, Z)
     yx = f // (2 * Z)
-    rank = lax.rem(f, 2 * Z) * Z + zl
     member = core * Z + zl
-
-    def in_column(p):
-        return (yx * (2 * Z) + p // Z, lax.rem(p, Z))
 
     def in_plane(p):
         return (p * (2 * Z) + lax.rem(f, 2 * Z), zl)
@@ -300,7 +295,6 @@
     def act_copy(peer, slot):
         return remote(act_out.at[peer], act_in.at[slot], act_s.at[peer], act_r.at[slot], in_block(peer))
 
-    others(2 * Z, member, lambda p: act_copy(p, member).start())
 
     first_chan = (lane - GROUPS) * per_group
     mask_b[...] = jnp.where((chan >= first_chan) & (chan < first_chan + per_group), 1.0, 0.0).astype(F32)
@@ -355,13 +349,15 @@
     for which, step in enumerate(steps):
         ring_copy(zh, which, step).start()
 
-    take_line(core, 0)
-
     @pl.when(takes_next)
     def _():
         landed(2, zl)
-        others(Z, zl, lambda p: block_copy(2, zl, next_line_s.at[p], (f, p)).start())
+        to_line(2, next_line_s, start)
         to_mate(2, zl, 1).start()
+
+    others(2 * Z, member, lambda p: act_copy(p, member).start())
+
+    take_line(core, 0)
 
     def from_mate(row, carry):
         landed(1 - core, row)
@@ -409,6 +405,10 @@
     grad_ref[...] = jnp.zeros((C, cells), F32)
     gradient((2,))
 
+
+    @pl.when(takes_next)
+    def _():
+        take_line(2, 1)
 
     for step in steps:
         ring_copy(block_at(step), 0, step).wait_recv()
@@ -449,14 +449,6 @@
                     j = low + n + 1 - row
                     partial[i * KERNEL + j] += product[n * width : (n + 1) * width]
 
-    @pl.when(takes_next)
-    def _():
-        def pass_next(row):
-            landed(2, row)
-            to_mate(2, row, 1).start()
-
-        others(Z, zl, pass_next)
-
     for lead in range(3):
         correlate(lead)
 
@@ -486,13 +478,14 @@
     scaled = shaped_grad * normed_ref[...]
     beta_sum = jnp.sum(shaped_grad[:, :half] + shaped_grad[:, half:], axis=1, keepdims=True)
     gamma_sum = jnp.sum(scaled[:, :half] + scaled[:, half:], axis=1, keepdims=True)
-    affine[yx, :, 0:C] = jnp.broadcast_to(gamma_sum, (C, LANES)).T[:1]
-    affine[yx, :, padded : padded + C] = jnp.broadcast_to(beta_sum, (C, LANES)).T[:1]
-    start_affine, recv_affine, sent_affine = exchange(affine, affine_s, affine_r, YX, yx, in_plane)
-    start_affine()
-    groups[rank] = jnp.sum(
+    sums[member, :, 0:C] = jnp.broadcast_to(gamma_sum, (C, LANES)).T[:1]
+    sums[member, :, padded : padded + C] = jnp.broadcast_to(beta_sum, (C, LANES)).T[:1]
+    sums[member, :, 2 * padded :] = jnp.sum(
         gain[0] * (mask_a[...] * beta_sum + mask_b[...] * gamma_sum), axis=0, keepdims=True
     )
+    start_sums, recv_sums, sent_sums = exchange(sums, sums_s, sums_r, 2 * Z, member, in_block)
+    start_sums()
+
     for lead in range(3, 5):
         correlate(lead)
 
@@ -522,31 +515,16 @@
     others(YX, yx, lambda p: plane_copy(p, yx).start())
     plane_in[yx] = jnp.zeros(plane_in.shape[1:], BF16)
 
-    start_groups, recv_groups, sent_groups = exchange(groups, groups_s, groups_r, column, rank, in_column)
-    start_groups()
-
-    recv_affine()
-    affine_rows = listed(affine)
-    mean_table[...] = affine_rows[:, 2 * padded : 2 * padded + GROUPS]
-    rstd_table[...] = affine_rows[:, 2 * padded + GROUPS : 2 * padded + 2 * GROUPS]
-    stores = [
-        pltpu.make_async_copy(source, target, store_sem.at[n])
-        for n, (source, target) in enumerate(
-            (
-                (mean_table, mean_ref),
-                (rstd_table, rstd_ref),
-                (act_grad, act_grad_ref),
-                (gamma_grad, gamma_grad_ref),
-                (beta_grad, beta_grad_ref),
-                (kernel_grad, kernel_grad_ref),
-            )
+    recv_sums()
+    clip_sums[zh] = jnp.sum(listed(sums), axis=0, keepdims=True)
+
+    def sums_copy(slot, which, step):
+        return remote(
+            clip_sums.at[slot], clip_sums.at[slot], clip_sums_s.at[which], clip_sums_r.at[slot], across_blocks(step)
         )
-    ]
-    stores[0].start()
-    stores[1].start()
-    affine_all[rank] = jnp.sum(affine_rows[:, : 2 * padded], axis=0, keepdims=True)
-    start_all, recv_all, sent_all = exchange(affine_all, all_s, all_r, column, rank, in_column)
-    start_all()
+
+    for which, step in enumerate(steps):
+        sums_copy(zh, which, step).start()
 
     others(YX, yx, lambda p: plane_copy(yx, p).wait_recv())
 
@@ -589,8 +567,14 @@
 
     lax.fori_loop(0, Z, send_part, 0)
 
-    recv_groups()
-    group_row = jnp.sum(listed(groups), axis=0, keepdims=True) / group_count
+    for step in steps:
+        sums_copy(block_at(step), 0, step).wait_recv()
+    clip_total = jnp.sum(listed(clip_sums), axis=0, keepdims=True)
+    affine[yx, :, : 2 * padded] = clip_total[:, : 2 * padded]
+    start_affine, recv_affine, sent_affine = exchange(affine, affine_s, affine_r, YX, yx, in_plane)
+    start_affine()
+
+    group_row = clip_total[:, 2 * padded :] / group_count
     first = jnp.sum(mask_a[...] * group_row, axis=1, keepdims=True)
     second = jnp.sum(mask_b[...] * group_row, axis=1, keepdims=True)
     for side in range(2):
@@ -598,10 +582,29 @@
         act_grad[:, side, :] = (
             rstd * (gain[0] * slope_ref[:, at] - first - normed_ref[:, at] * second)
         ).astype(BF16)
+
+    stores = [
+        pltpu.make_async_copy(source, target, store_sem.at[n])
+        for n, (source, target) in enumerate(
+            (
+                (act_grad, act_grad_ref),
+                (mean_table, mean_ref),
+                (rstd_table, rstd_ref),
+                (gamma_grad, gamma_grad_ref),
+                (beta_grad, beta_grad_ref),
+                (kernel_grad, kernel_grad_ref),
+            )
+        )
+    ]
+    stores[0].start()
+
+    recv_affine()
+    affine_rows = listed(affine)
+    mean_table[...] = affine_rows[:, 2 * padded : 2 * padded + GROUPS]
+    rstd_table[...] = affine_rows[:, 2 * padded + GROUPS : 2 * padded + 2 * GROUPS]
+    stores[1].start()
     stores[2].start()
-
-    recv_all()
-    totals = jnp.sum(listed(affine_all), axis=0, keepdims=True) * scale
+    totals = jnp.sum(affine_rows[:, : 2 * padded], axis=0, keepdims=True) * scale
     gamma_grad[...] = totals[:, :C].reshape(C)
     beta_grad[...] = totals[:, padded : padded + C].reshape(C)
     stores[3].start()
@@ -610,9 +613,10 @@
     sent_stats()
     for which, step in enumerate(steps):
         ring_copy(zh, which, step).wait_send()
-    sent_groups()
+    sent_sums()
+    for which, step in enumerate(steps):
+        sums_copy(zh, which, step).wait_send()
     sent_affine()
-    sent_all()
 
     @pl.when(gives_next)
     def _():
@@ -629,7 +633,8 @@
 
     @pl.when(takes_next)
     def _():
-        others(Z, zl, lambda p: block_copy(2, zl, next_line_s.at[p], (f, p)).wait_send())
+        to_line(2, next_line_s, wait_send)
+        passed(2, 1, wait_send)
 
         def next_sent(row, carry):
             to_mate(2, row, 1).wait_send()
@@ -708,9 +713,9 @@
         pltpu.VMEM((C, cells), F32),
         pltpu.VMEM((2 * Z, 1, LANES), F32),
         pltpu.VMEM((Z, 1, LANES), F32),
-        pltpu.VMEM((column, 1, LANES), F32),
+        pltpu.VMEM((2 * Z, 1, 2 * padded + LANES), F32),
+        pltpu.VMEM((Z, 1, 2 * padded + LANES), F32),
         pltpu.VMEM((YX, 1, 2 * padded + LANES), F32),
-        pltpu.VMEM((column, 1, 2 * padded), F32),
         pltpu.VMEM((3, Z, O, cells), BF16),
         pltpu.VMEM((5, Z + 2, KERNEL * LANES, cells), BF16),
         pltpu.VMEM((KERNEL**3, LANES, C), BF16),
@@ -735,14 +740,14 @@
         dma((6,)),
         dma((2 * Z,)),
         dma((2 * Z,)),
-        dma((3,)),
         dma((Z,)),
-        dma((column,)),
-        dma((column,)),
+        dma((Z,)),
+        dma((2 * Z,)),
+        dma((2 * Z,)),
+        dma((Z,)),
+        dma((Z,)),
         dma((YX,)),
         dma((YX,)),
-        dma((column,)),
-        dma((column,)),
         dma((Z,)),
         dma((2, Z)),
         dma((1,)),

time: 55.7 us -> 53.5 us (0.961)
  Pallas kernels: 54.9 us -> 52.7 us
    pallas_call x1, Pallas kernels: 53.1 us -> 51 us  [on_device(): pl.pallas_call(functools.partial(body, sizes), out_shape=outputs, in_spec...]
where the time goes in v2:
time: 53.5 us; the launch traced here: 53.3 us
  Pallas kernels  52.7 us (99%)
  between operations  0.64 us (1%)
    pallas_call x1, Pallas kernels, on_device(): pl.pallas_call(functools.partial(body, sizes), out_shape=outputs, in_spec...  51 us
    pallas_call x1, Pallas kernels, on_device(): pl.pallas_call(hand_over, out_shape=outputs, in_specs=[hbm] * 6, out_spec...  1.72 us

profile of v2, /device:TPU:1, one launch (start us, length us, event | category | flops | bytes accessed | tf_op | source)
XLA Modules:
  0.0 53.3 jit_solution(16040359898988039791)
XLA Ops:
  0.6 51.0 %unit_backward.1 = (bf16[384,2,128]{2,1,0:T(2,128)(2,1)}, f32[27,72]{1,0:T(8,128)}, f32[384]{0:T(512)}, f32[384]{0:T(512)}, f32[16,32]{1,0:T(8,128)}, /*index=5*/f32[16,32]{1,0:T(8,128)}) custom-call(bf16[384,2,128]{2,1,0:T(2,128)(2,1)} %bitcast.5, bf16[96,2,128]{2,1,0:T(2,128)(2,1)} %bitcast.6, bf16[27,96,384]{2,1,0:T(8,128)(2,1)} %kernel_ref.1, ...), custom_call_target="tpu_custom_call" | custom-call | tf_op jit(solution)/shard_map/unit_backward/pallas_call | solution.py:764
  51.6 1.7 %hand_over.1 = (bf16[384,2,128]{2,1,0:T(2,128)(2,1)}, f32[27,72]{1,0:T(8,128)}, f32[384]{0:T(512)}, f32[384]{0:T(512)}, f32[16,32]{1,0:T(8,128)}, /*index=5*/f32[16,32]{1,0:T(8,128)}) custom-call(bf16[384,2,128]{2,1,0:T(2,128)(2,1)} %get-tuple-element.18.refs_0_, f32[27,72]{1,0:T(8,128)} %get-tuple-element.19.refs_1_, f32[384]{0:T(512)} %get-tuple-element.20.refs_2_, ...), custom_call_target="tpu_custom_call" | custom-call | tf_op jit(solution)/shard_map/hand_over/pallas_call | solution.py:781

commit v3 on v2

--- a/solution.py
+++ b/solution.py
@@ -101,6 +101,8 @@
     plane_in,
     column_out,
     column_in,
+    line_ready,
+    far_ready,
     load_sem,
     store_sem,
     stats_s,
@@ -151,17 +153,25 @@
         return (yx * (2 * Z) + lax.rem(zh + step + Z, Z) * 2 + core, zl)
 
     partner = (yx * (2 * Z) + lax.rem(zh + 2 * core - 1 + Z, Z) * 2 + 1 - core, zl)
-    steps = [Z // 2] + [step for n in range(1, Z // 2) for step in (n, -n)]
+    beside = (1,) if Z == 2 else (1, -1)
+    steps = beside if Z == 2 else (1, -1, 2)
 
     barrier = pltpu.get_barrier_semaphore()
 
     def greet(device):
         pl.semaphore_signal(barrier, inc=1, device_id=device, device_id_type=MESH)
 
-    for step in steps:
+    for step in beside:
         greet(across_blocks(step))
     greet(partner)
-    others(YX, yx, lambda p: greet(in_plane(p)), True)
+    X = 4 if YX % 4 == 0 else YX
+    x, y = lax.rem(yx, X), yx // X
+
+    def along_x(p):
+        return in_plane(y * X + p)
+
+    others(X, x, lambda p: greet(along_x(p)), True)
+    others(YX // X, y, lambda p: greet(in_plane(p * X + x)), True)
     others(2 * Z, member, lambda p: greet(in_block(p)))
 
     loads = [
@@ -211,7 +221,10 @@
     act_out[...] = ordered.reshape(act_out.shape)
     act_in[member] = act_out[member]
 
-    pl.semaphore_wait(barrier, len(steps) + 1 + YX - 1 + 2 * Z - 1)
+    pl.semaphore_wait(barrier, len(beside) + 1 + X - 1 + YX // X - 1 + 2 * Z - 1)
+
+    if Z > 2:
+        pl.semaphore_signal(far_ready, inc=1, device_id=across_blocks(-1), device_id_type=MESH)
 
     def block_copy(pair, row, send, device):
         ref = blocks.at[pair, row]
@@ -295,6 +308,8 @@
     def act_copy(peer, slot):
         return remote(act_out.at[peer], act_in.at[slot], act_s.at[peer], act_r.at[slot], in_block(peer))
 
+
+    others(X, x, lambda p: pl.semaphore_signal(line_ready, inc=1, device_id=along_x(p), device_id_type=MESH))
 
     first_chan = (lane - GROUPS) * per_group
     mask_b[...] = jnp.where((chan >= first_chan) & (chan < first_chan + per_group), 1.0, 0.0).astype(F32)
@@ -328,6 +343,9 @@
         for k in range(KERNEL):
             slabs[:, 1 : Z + 1, k * LANES + O : (k + 1) * LANES, :] = jnp.zeros((5, Z, LANES - O, cells), BF16)
 
+    partial[...] = jnp.zeros(partial.shape, F32)
+    by_owner[...] = jnp.zeros(by_owner.shape, F32)
+
     lane_row = lax.broadcasted_iota(jnp.int32, (1, LANES), 1)
 
     def combined(rows, cells_of_one):
@@ -347,6 +365,8 @@
         return lax.rem(zh + step + Z, Z)
 
     for which, step in enumerate(steps):
+        if step == 2:
+            pl.semaphore_wait(far_ready, 1)
         ring_copy(zh, which, step).start()
 
     @pl.when(takes_next)
@@ -410,6 +430,12 @@
     def _():
         take_line(2, 1)
 
+    @pl.when(core == 1)
+    def _():
+        fill(range(4, 6))
+
+    gradient((0, 1))
+
     for step in steps:
         ring_copy(block_at(step), 0, step).wait_recv()
     mean_row, squares_row = combined(listed(ring), 2 * Z * per_group * cells)
@@ -429,7 +455,6 @@
         shaped = (act_in[slot].astype(F32) - own_mean) * own_rstd * own_gamma + own_beta
         act_in[slot] = (shaped / (1.0 + jnp.exp(-shaped))).astype(BF16)
 
-    partial[...] = jnp.zeros(partial.shape, F32)
 
     def correlate(lead):
         for row in range(Z):
@@ -462,17 +487,6 @@
         normed_ref[:, at] = normed
         slope_ref[:, at] = sig * (1.0 + shaped * (1.0 - sig))
 
-    @pl.when((core == 0) & (zh < Z - 1))
-    def _():
-        def next_from_mate(row, carry):
-            landed(2, row)
-            return carry
-
-        lax.fori_loop(0, Z, next_from_mate, 0)
-
-    fill(range(4, 6))
-
-    gradient((0, 1))
     shaped_grad = grad_ref[...] * slope_ref[...]
     slope_ref[...] = shaped_grad
     scaled = shaped_grad * normed_ref[...]
@@ -486,19 +500,17 @@
     start_sums, recv_sums, sent_sums = exchange(sums, sums_s, sums_r, 2 * Z, member, in_block)
     start_sums()
 
-    for lead in range(3, 5):
-        correlate(lead)
-
-    by_owner[...] = jnp.zeros(by_owner.shape, F32)
-
     tile_rows = min(8, YX)
     tiles = YX // tile_rows
 
-    def arrange(tile, carry):
+    def arrange(lags):
+        lax.fori_loop(0, 3 * tiles, functools.partial(arrange_tile, lags), 0)
+
+    def arrange_tile(lags, tile, carry):
         c = tile // tiles
         first_place = lax.rem(tile, tiles) * tile_rows
         at = pl.ds(pl.multiple_of(tile * tile_rows, tile_rows), tile_rows)
-        for ij in range(KERNEL**2):
+        for ij in [i * KERNEL + j for i in lags for j in range(KERNEL)]:
             for k in range(KERNEL):
                 tap = ij * KERNEL + k
                 values = partial[ij, at, k * LANES : (k + 1) * LANES]
@@ -506,12 +518,31 @@
                     by_owner[(first_place + row) * 3 + c, tap : tap + 1, :] = values[row : row + 1]
         return carry
 
-    lax.fori_loop(0, 3 * tiles, arrange, 0)
+    arrange((2,))
+
+    @pl.when((core == 0) & (zh < Z - 1))
+    def _():
+        def next_from_mate(row, carry):
+            landed(2, row)
+            return carry
+
+        lax.fori_loop(0, Z, next_from_mate, 0)
+
+    @pl.when(core == 0)
+    def _():
+        fill(range(4, 6))
+
+    for lead in range(3, 5):
+        correlate(lead)
+
+
+    arrange((0, 1))
     plane_out[...] = by_owner[...].astype(BF16).reshape(plane_out.shape)
 
     def plane_copy(peer, slot):
         return remote(plane_out.at[peer], plane_in.at[slot], plane_s.at[peer], plane_r.at[slot], in_plane(peer))
 
+    pl.semaphore_wait(line_ready, X - 1)
     others(YX, yx, lambda p: plane_copy(p, yx).start())
     plane_in[yx] = jnp.zeros(plane_in.shape[1:], BF16)
 
@@ -736,6 +767,8 @@
         pltpu.VMEM((YX, 3, 32, LANES), BF16),
         pltpu.VMEM((Z, 32, LANES), F32),
         pltpu.VMEM((Z, 32, LANES), F32),
+        pltpu.SemaphoreType.REGULAR,
+        pltpu.SemaphoreType.REGULAR,
         dma((5,)),
         dma((6,)),
         dma((2 * Z,)),

time: 53.5 us -> 53.1 us (level)
  no operation moved by 1% of the time
where the time goes in v3:
time: 53.1 us; the launch traced here: 52.9 us
  Pallas kernels  52.3 us (98%)
  between operations  0.64 us (1%)
    pallas_call x1, Pallas kernels, on_device(): pl.pallas_call(functools.partial(body, sizes), out_shape=outputs, in_spec...  50.5 us
    pallas_call x1, Pallas kernels, on_device(): pl.pallas_call(hand_over, out_shape=outputs, in_specs=[hbm] * 6, out_spec...  1.72 us

profile of v3, /device:TPU:1, one launch (start us, length us, event | category | flops | bytes accessed | tf_op | source)
XLA Modules:
  0.0 52.9 jit_solution(9152539853665696111)
XLA Ops:
  0.6 50.5 %unit_backward.1 = (bf16[384,2,128]{2,1,0:T(2,128)(2,1)}, f32[27,72]{1,0:T(8,128)}, f32[384]{0:T(512)}, f32[384]{0:T(512)}, f32[16,32]{1,0:T(8,128)}, /*index=5*/f32[16,32]{1,0:T(8,128)}) custom-call(bf16[384,2,128]{2,1,0:T(2,128)(2,1)} %bitcast.5, bf16[96,2,128]{2,1,0:T(2,128)(2,1)} %bitcast.6, bf16[27,96,384]{2,1,0:T(8,128)(2,1)} %kernel_ref.1, ...), custom_call_target="tpu_custom_call" | custom-call | tf_op jit(solution)/shard_map/unit_backward/pallas_call | solution.py:797
  51.2 1.7 %hand_over.1 = (bf16[384,2,128]{2,1,0:T(2,128)(2,1)}, f32[27,72]{1,0:T(8,128)}, f32[384]{0:T(512)}, f32[384]{0:T(512)}, f32[16,32]{1,0:T(8,128)}, /*index=5*/f32[16,32]{1,0:T(8,128)}) custom-call(bf16[384,2,128]{2,1,0:T(2,128)(2,1)} %get-tuple-element.18.refs_0_, f32[27,72]{1,0:T(8,128)} %get-tuple-element.19.refs_1_, f32[384]{0:T(512)} %get-tuple-element.20.refs_2_, ...), custom_call_target="tpu_custom_call" | custom-call | tf_op jit(solution)/shard_map/hand_over/pallas_call | solution.py:814

commit v4 on v3

--- a/solution.py
+++ b/solution.py
@@ -596,7 +596,8 @@
 
         return carry
 
-    lax.fori_loop(0, Z, send_part, 0)
+    for step in range(1, Z + 1):
+        send_part(lax.rem(zl + step, Z), 0)
 
     for step in steps:
         sums_copy(block_at(step), 0, step).wait_recv()

time: 53.1 us -> 53.1 us (level)
  no operation moved by 1% of the time
where the time goes in v4:
time: 53.1 us; the launch traced here: 52.9 us
  Pallas kernels  52.3 us (98%)
  between operations  0.64 us (1%)
    pallas_call x1, Pallas kernels, on_device(): pl.pallas_call(functools.partial(body, sizes), out_shape=outputs, in_spec...  50.5 us
    pallas_call x1, Pallas kernels, on_device(): pl.pallas_call(hand_over, out_shape=outputs, in_specs=[hbm] * 6, out_spec...  1.72 us

profile of v4, /device:TPU:1, one launch (start us, length us, event | category | flops | bytes accessed | tf_op | source)
XLA Modules:
  0.0 52.9 jit_solution(3321618722616887128)
XLA Ops:
  0.6 50.5 %unit_backward.1 = (bf16[384,2,128]{2,1,0:T(2,128)(2,1)}, f32[27,72]{1,0:T(8,128)}, f32[384]{0:T(512)}, f32[384]{0:T(512)}, f32[16,32]{1,0:T(8,128)}, /*index=5*/f32[16,32]{1,0:T(8,128)}) custom-call(bf16[384,2,128]{2,1,0:T(2,128)(2,1)} %bitcast.5, bf16[96,2,128]{2,1,0:T(2,128)(2,1)} %bitcast.6, bf16[27,96,384]{2,1,0:T(8,128)(2,1)} %kernel_ref.1, ...), custom_call_target="tpu_custom_call" | custom-call | tf_op jit(solution)/shard_map/unit_backward/pallas_call | solution.py:798
  51.2 1.7 %hand_over.1 = (bf16[384,2,128]{2,1,0:T(2,128)(2,1)}, f32[27,72]{1,0:T(8,128)}, f32[384]{0:T(512)}, f32[384]{0:T(512)}, f32[16,32]{1,0:T(8,128)}, /*index=5*/f32[16,32]{1,0:T(8,128)}) custom-call(bf16[384,2,128]{2,1,0:T(2,128)(2,1)} %get-tuple-element.18.refs_0_, f32[27,72]{1,0:T(8,128)} %get-tuple-element.19.refs_1_, f32[384]{0:T(512)} %get-tuple-element.20.refs_2_, ...), custom_call_target="tpu_custom_call" | custom-call | tf_op jit(solution)/shard_map/hand_over/pallas_call | solution.py:815
